TPU v7x, 32 devices: a whole 2x2x4 slice. The times are simulated.
32 devices in a mesh: groups: 2 (over y), panels: 8 (over z, core), rhs: 2 (over x).
Axes of the slice: x: 2, y: 2, z: 4, core: 2. Of those that a mesh axis runs over, the one named last changes fastest.
Arguments:
- incident: bfloat16 [32, 65536], P('rhs', ('groups', 'panels')), parts along dimension 1, may hold values from -16 to 16
- tree_order: int32 [65536], P(('groups', 'panels')), parts along dimension 0, may hold values from 0 to 32767, as said below
- near_rows: int32 [3072], P(('groups', 'panels', 'rhs')), parts along dimension 0, may hold values from 0 to 32, as said below
- near_sources: int32 [3072], P(('groups', 'panels', 'rhs')), parts along dimension 0, may hold values from 0 to 255, as said below
- near_blocks: bfloat16 [3072, 128, 128], P(('groups', 'panels', 'rhs')), parts along dimension 0, may hold values from -0.21875 to 0.21875
- far_rows: int32 [1472], P(('groups', 'panels', 'rhs')), parts along dimension 0, may hold values from 0 to 32, as said below
- far_sources: int32 [1472], P(('groups', 'panels', 'rhs')), parts along dimension 0, may hold values from 0 to 255, as said below
- far_left: bfloat16 [1472, 16, 128], P(('groups', 'panels', 'rhs')), parts along dimension 0, may hold values from -0.875 to 0.875
- far_right: bfloat16 [1472, 16, 128], P(('groups', 'panels', 'rhs')), parts along dimension 0, may hold values from -0.5 to 0.5
Outputs:
- first_image: float32 [32, 65536], P('rhs', ('groups', 'panels')), parts along dimension 1
- second_image: float32 [32, 65536], P('rhs', ('groups', 'panels')), parts along dimension 1
There are 2 independent parts, one for each index of `groups`. A program takes and returns all parts, laid end to end along the dimension named above; each array names one. Nothing has to cross between parts.
Inputs may be any that keep to these rules, and one draw needn't show every extreme that they name: `tree_order`: tree positions of one owner's range of 4096 panels name panels of that same range, each once. `near_rows`: 32 marks padding; padding stands at the end of each device's list of 96 entries, and some device's list has none. `near_sources`: A live entry's source cluster lies within 2 clusters of its row cluster in global order; every entry's source lies within 2 clusters of its owner's range. `far_rows`: 32 marks padding; padding stands at the end of each device's list of 46 entries, and some device's list has none. `far_sources`: each device's far list names exactly 2 source clusters of every other owner and 32 of its own owner, in any order.
All inputs are finite; a program needn't handle non-finite values.
Results may differ from a plain program's by a relative error of at most 0.0041.
Values may be sent and summed in bfloat16 or wider, within the bound.
A program may use at most 64 MiB of HBM per device.

v0:
```python
import jax
import jax.numpy as jnp
from jax import lax
from jax.sharding import PartitionSpec as P

NEAR_REACH = 2
FAR_PEER = 2


def with_halo(x, sides, width):
    for axis, dim in sides:
        size, length = (lax.axis_size(axis), x.shape[dim])
        up = [(i, (i + 1) % size) for i in range(size - 1)]
        down = [(j, i) for i, j in up]
        last = lax.slice_in_dim(x, length - width, length, axis=dim)
        leading = lax.slice_in_dim(x, 0, width, axis=dim)
        before = lax.ppermute(last, axis, up)
        after = lax.ppermute(leading, axis, down)
        x = jnp.concatenate([before, x, after], axis=dim)
    return x


def on_device(
    incident,
    tree_order,
    near_rows,
    near_sources,
    near_blocks,
    far_rows,
    far_sources,
    far_left,
    far_right,
):
    owner = lax.axis_index("panels")
    owners = lax.axis_size("panels")
    block_size = near_blocks.shape[1]
    panel_count = incident.shape[1]
    cluster_count = panel_count // block_size
    headings = incident.shape[0] * lax.axis_size("rhs")
    total_panels = panel_count * owners
    reach = NEAR_REACH
    capacity = FAR_PEER
    highest = lax.Precision.HIGHEST
    local_order = tree_order - owner * panel_count
    tree = jnp.take(incident, local_order, axis=1)
    cluster_ids = jnp.arange(cluster_count, dtype=jnp.int32)
    near_hot = (near_rows[:, None] == cluster_ids[None, :]).astype(jnp.float32)
    far_hot = (far_rows[:, None] == cluster_ids[None, :]).astype(jnp.float32)
    near_index = near_sources - (owner * cluster_count - reach)
    target = far_sources // cluster_count
    within = far_sources % cluster_count
    remote = target != owner
    peer_ids = jnp.arange(owners, dtype=jnp.int32)
    peer_hot = ((target[:, None] == peer_ids[None, :]) & remote[:, None]).astype(jnp.int32)
    earlier = jnp.cumsum(peer_hot, axis=0) - peer_hot
    slot_rank = jnp.sum(earlier * peer_hot, axis=1)
    send_peer = jnp.where(remote, target, owners)
    asks = (
        jnp.zeros((owners, capacity), jnp.int32).at[send_peer, slot_rank].set(within, mode="drop")
    )
    asked = lax.all_to_all(asks, "panels", split_axis=0, concat_axis=0, tiled=True)

    def operate(field):
        every = lax.all_gather(field, "rhs", axis=0, tiled=True)
        widened = with_halo(every, (("panels", 1),), reach * block_size)
        near_segments = widened.reshape(headings, cluster_count + 2 * reach, block_size)
        own_segments = every.reshape(headings, cluster_count, block_size)
        near_input = near_segments[:, near_index]
        served = own_segments[:, asked]
        local_input = own_segments[:, within]
        arrived = lax.all_to_all(served, "panels", split_axis=1, concat_axis=1, tiled=True)
        far_input = jnp.where(remote[None, :, None], arrived[:, target, slot_rank], local_input)
        far_coef = jnp.einsum(
            "emj,hej->hem", far_right, far_input, preferred_element_type=jnp.float32
        ).astype(jnp.bfloat16)
        near_terms = jnp.einsum(
            "ekj,hej->hek", near_blocks, near_input, preferred_element_type=jnp.float32
        )
        far_terms = jnp.einsum(
            "emk,hem->hek", far_left, far_coef, preferred_element_type=jnp.float32
        )
        placed = jnp.einsum("ec,hek->hck", near_hot, near_terms, precision=highest)
        placed = placed + jnp.einsum("ec,hek->hck", far_hot, far_terms, precision=highest)
        return lax.psum_scatter(
            placed.reshape(field.shape[0] * lax.axis_size("rhs"), panel_count),
            "rhs",
            scatter_dimension=0,
            tiled=True,
        )

    first_tree = operate(tree)
    squares = jnp.sum(first_tree * first_tree, axis=1)
    totals = lax.psum(squares, "panels")
    scale = lax.rsqrt(totals / total_panels + 1e-06)
    normed = (first_tree * scale[:, None]).astype(jnp.bfloat16)
    second_tree = operate(normed)
    both = jnp.concatenate([first_tree, second_tree], axis=0)
    images = jnp.zeros_like(both).at[:, local_order].set(both)
    rows = first_tree.shape[0]
    return (images[:rows], images[rows:])


def solution(mesh):
    in_specs = (
        P("rhs", ("groups", "panels")),
        P(("groups", "panels")),
        P(("groups", "panels", "rhs")),
        P(("groups", "panels", "rhs")),
        P(("groups", "panels", "rhs"), None, None),
        P(("groups", "panels", "rhs")),
        P(("groups", "panels", "rhs")),
        P(("groups", "panels", "rhs"), None, None),
        P(("groups", "panels", "rhs"), None, None),
    )
    out_specs = (P("rhs", ("groups", "panels")), P("rhs", ("groups", "panels")))
    return jax.shard_map(
        on_device, mesh=mesh, in_specs=in_specs, out_specs=out_specs, check_vma=False
    )
```

profile of v0, /device:TPU:0, one launch (start us, length us, event | category | flops | bytes accessed | tf_op | source)
XLA Modules:
  0.0 211.1 jit_solution(16275863670714022531)
XLA Ops:
  9.2 2.8 %scatter_fusion = s32[8,2]{0,1:T(2,128)S(1)} fusion(s32[8,2]{0,1:T(2,128)S(1)} %broadcast.81, s32[46]{0:T(128)S(1)} %get-tuple-element.27, s32[46]{0:T(128)S(1)} %get-tuple-element.15), kind=kCustom, calls=%fused_computation.9 | custom fusion | bytes 920 | tf_op jit(solution)/shard_map/scatter | solution.py:59
  12.6 6.3 %all-to-all-start = ((s32[8,1,2]{2,1,0:T(1,128)}), s32[8,1,2]{2,1,0:T(1,128)S(1)}, u32[]{:S(2)}, u32[]{:S(2)}) async-start(s32[8,1,2]{2,1,0:T(1,128)} %copy.88), calls=%async_computation | async-start | bytes 8192 | tf_op jit(solution)/shard_map/all_to_all | solution.py:61
  19.7 2.2 %copy.84 = bf16[16,4096]{0,1:T(8,128)(2,1)} copy(bf16[16,4096]{1,0:T(8,128)(2,1)} %param.9) | data formatting | bytes 262144 | tf_op args[0]
  21.9 15.7 %gather_fusion = bf16[4096,16]{1,0:T(8,128)(2,1)} fusion(bf16[16,4096]{0,1:T(8,128)(2,1)} %copy.84, s32[4096]{0:T(1024)S(1)} %broadcast_clamp_fusion), kind=kCustom, calls=%fused_computation | custom fusion | bytes 278528 | tf_op jit(solution)/shard_map/jit(_take)/gather | solution.py:45
  37.6 4.2 %select_bitcast_fusion = bf16[16,4096]{0,1:T(8,128)(2,1)} fusion(bf16[4096,16]{1,0:T(8,128)(2,1)} %gather_fusion, pred[4096]{0:T(1024)(128)(4,1)S(1)} %get-tuple-element.18), kind=kLoop, calls=%fused_computation.28 | loop fusion | flops 65536 | bytes 266240 | tf_op jit(solution)/shard_map/jit(_take)/select_n | solution.py:45
  43.4 6.6 %all_gather.6 = bf16[32,4096]{1,0:T(8,128)(2,1)S(1)} all-gather(bf16[16,4096]{1,0:T(8,128)(2,1)S(1)} %copy.85), channel_id=1, replica_groups=mesh['groups'=2,'panels'=8,'rhs'=2] {'rhs'}, dimensions={0}, use_global_device_ids=true | all-gather | bytes 393216 | tf_op jit(solution)/shard_map/all_gather | solution.py:64
  55.9 7.4 %all-to-all-start.1 = ((bf16[32,8,2,128]{3,0,2,1:T(8,128)(2,1)}), bf16[32,8,2,128]{3,0,2,1:T(8,128)(2,1)}, u32[]{:S(2)}, u32[]{:S(2)}) async-start(bf16[32,8,2,128]{3,0,2,1:T(8,128)(2,1)} %bitcast.10), calls=%async_computation.1 | async-start | bytes 262144 | tf_op jit(solution)/shard_map/all_to_all | solution.py:71
  65.9 4.0 %convolution_bitcast_fusion.1 = f32[32,96,128]{2,0,1:T(8,128)} fusion(bf16[96,128,128]{2,1,0:T(8,128)(2,1)S(1)} %copy-done, bf16[96,32,128]{2,1,0:T(8,128)(2,1)} %gather_fusion.1), kind=kOutput, calls=%fused_computation.17 | convolution fusion | flops 100663296 | bytes 5505024 | tf_op jit(solution)/shard_map/ekj,hej->hek/dot_general | solution.py:76
  71.9 2.6 %convolution_bitcast_fusion.3 = f32[32,46,128]{2,0,1:T(8,128)} fusion(bf16[46,16,128]{2,1,0:T(8,128)(2,1)} %param.16, bf16[46,16,128]{2,1,0:T(8,128)(2,1)} %param.17, bf16[46,32,128]{2,1,0:T(8,128)(2,1)S(1)} %gather_fusion.3, bf16[46,32,128]{2,1,0:T(8,128)(2,1)} %gather_fusion.4, pred[46]{0:T(512)(128)(4,1)S(1)} %get-tuple-element.16), kind=kOutput, calls=%fused_computation.19 | convolution fusion | flops 12270592 | bytes 1884206 | tf_op jit(solution)/shard_map/emk,hem->hek/dot_general | solution.py:79
  74.5 2.0 fusion.24
  76.5 3.7 %fusion.7 = f32[32,32,128]{2,1,0:T(8,128)} fusion(f32[32,128,32]{1,2,0:T(8,128)S(1)} %fusion.24, f32[32,96,128]{2,0,1:T(8,128)} %convolution_bitcast_fusion.1, s32[96]{0:T(128)} %param.11), kind=kOutput, calls=%fused_computation.21 | convolution fusion | flops 151129088 | bytes 2621824 | tf_op jit(solution)/shard_map/ec,hek->hck/dot_general | solution.py:82
  80.2 3.0 %copy.107 = f32[32,32,128]{0,2,1:T(8,128)} copy(f32[32,32,128]{2,1,0:T(8,128)} %fusion.7) | data formatting | bytes 1048576 | tf_op jit(solution)/shard_map/reshape | solution.py:85
  83.2 3.0 %copy.109 = f32[32,4096]{1,0:T(8,128)} copy(f32[32,4096]{0,1:T(8,128)} %bitcast.112) | data formatting | bytes 1048576
  86.2 15.9 %reduce-scatter.7.cloned.1.call-done = f32[16,4096]{1,0:T(8,128)} async-done(((f32[32,4096]{1,0:T(8,128)}), f32[16,4096]{1,0:T(8,128)}) %reduce-scatter.7.cloned.1.call-update) | async-done | bytes 262160 | tf_op jit(solution)/shard_map/reduce_scatter | solution.py:84
  102.1 3.0 %copy.110 = f32[16,4096]{0,1:T(8,128)} copy(f32[16,4096]{1,0:T(8,128)} %reduce-scatter.7.cloned.1.call-done) | data formatting | bytes 524288
  105.1 2.1 %multiply_reduce_fusion = f32[16]{0:T(128)S(1)} fusion(f32[16,4096]{0,1:T(8,128)} %copy.110), kind=kLoop, calls=%fused_computation.11 | loop fusion | flops 131056 | bytes 262208 | tf_op jit(solution)/shard_map/reduce_sum | solution.py:92
  107.2 16.3 %psum.7 = f32[16]{0:T(128)S(1)} all-reduce(f32[16]{0:T(128)S(1)} %multiply_reduce_fusion), channel_id=1, replica_groups=mesh['groups'=2,'panels'=8,'rhs'=2] {'panels'}, use_global_device_ids=true, to_apply=%region_5.6 | all-reduce | flops 16 | bytes 128 | tf_op jit(solution)/shard_map/psum | solution.py:93
  123.7 5.6 %all_gather.7 = bf16[32,4096]{1,0:T(8,128)(2,1)S(1)} all-gather(bf16[16,4096]{1,0:T(8,128)(2,1)S(1)} %multiply_convert_fusion), channel_id=1, replica_groups=mesh['groups'=2,'panels'=8,'rhs'=2] {'rhs'}, dimensions={0}, use_global_device_ids=true | all-gather | bytes 393216 | tf_op jit(solution)/shard_map/all_gather | solution.py:64
  134.7 4.0 %all-to-all-start.2 = ((bf16[32,8,2,128]{3,0,2,1:T(8,128)(2,1)}), bf16[32,8,2,128]{3,0,2,1:T(8,128)(2,1)}, u32[]{:S(2)}, u32[]{:S(2)}) async-start(bf16[32,8,2,128]{3,0,2,1:T(8,128)(2,1)} %bitcast.22), calls=%async_computation.2 | async-start | bytes 262144 | tf_op jit(solution)/shard_map/all_to_all | solution.py:71
  141.5 4.0 %convolution_bitcast_fusion = f32[32,96,128]{2,0,1:T(8,128)} fusion(bf16[96,128,128]{2,1,0:T(8,128)(2,1)S(1)} %copy-done, bf16[96,32,128]{2,1,0:T(8,128)(2,1)} %gather_fusion.5), kind=kOutput, calls=%fused_computation.16 | convolution fusion | flops 100663296 | bytes 5505024 | tf_op jit(solution)/shard_map/ekj,hej->hek/dot_general | solution.py:76
  145.5 1.8 gather_fusion.7
  147.3 2.6 %convolution_bitcast_fusion.2 = f32[32,46,128]{2,0,1:T(8,128)} fusion(bf16[46,16,128]{2,1,0:T(8,128)(2,1)} %param.16, bf16[46,16,128]{2,1,0:T(8,128)(2,1)} %param.17, bf16[46,32,128]{2,1,0:T(8,128)(2,1)S(1)} %gather_fusion.7, bf16[46,32,128]{2,1,0:T(8,128)(2,1)} %gather_fusion.8, pred[46]{0:T(512)(128)(4,1)S(1)} %get-tuple-element.16), kind=kOutput, calls=%fused_computation.18 | convolution fusion | flops 12270592 | bytes 1884206 | tf_op jit(solution)/shard_map/emk,hem->hek/dot_general | solution.py:79
  149.9 2.0 fusion.22
  151.9 3.7 %fusion.13 = f32[32,32,128]{2,1,0:T(8,128)} fusion(f32[32,128,32]{1,2,0:T(8,128)S(1)} %fusion.22, f32[32,96,128]{2,0,1:T(8,128)} %convolution_bitcast_fusion, s32[96]{0:T(128)S(1)} %copy-done.7), kind=kOutput, calls=%fused_computation.23 | convolution fusion | flops 151129088 | bytes 2621824 | tf_op jit(solution)/shard_map/ec,hek->hck/dot_general | solution.py:82
  155.6 3.0 %copy.108 = f32[32,32,128]{0,2,1:T(8,128)} copy(f32[32,32,128]{2,1,0:T(8,128)} %fusion.13) | data formatting | bytes 1048576 | tf_op jit(solution)/shard_map/reshape | solution.py:85
  158.6 3.0 %copy.111 = f32[32,4096]{1,0:T(8,128)} copy(f32[32,4096]{0,1:T(8,128)} %bitcast.113) | data formatting | bytes 1048576
  161.7 14.9 %reduce-scatter.9.cloned.1.call-done = f32[16,4096]{1,0:T(8,128)} async-done(((f32[32,4096]{1,0:T(8,128)}), f32[16,4096]{1,0:T(8,128)}) %reduce-scatter.9.cloned.1.call-update) | async-done | bytes 262160 | tf_op jit(solution)/shard_map/reduce_scatter | solution.py:84
  178.3 3.0 %copy.104 = f32[4096,32]{1,0:T(8,128)} copy(f32[4096,32]{0,1:T(8,128)} %maximum_bitcast_fusion) | data formatting | bytes 1048576 | tf_op jit(solution)/shard_map/concatenate | solution.py:97
  181.3 12.3 %scatter_custom_fusion.1 = f32[32,4096]{0,1:T(8,128)} fusion(s32[4096]{0:T(1024)S(1)} %get-tuple-element.19, f32[4096,32]{1,0:T(8,128)} %copy.104, f32[]{:T(128)} %constant.37.clone.1), kind=kCustom, calls=%fused_computation.29 | custom fusion | bytes 524800 | tf_op jit(solution)/shard_map/scatter | solution.py:98
  193.6 4.9 %fusion.58 = (f32[16,4096]{0,1:T(8,128)}, f32[16,4096]{0,1:T(8,128)}) fusion(f32[32,4096]{0,1:T(8,128)} %scatter_custom_fusion.1), kind=kLoop, calls=%fused_computation.93 | loop fusion | bytes 1048576 | tf_op jit(solution)/shard_map/slice | solution.py:100
  198.5 2.9 %copy.106 = f32[16,4096]{1,0:T(8,128)} copy(f32[16,4096]{0,1:T(8,128)} %get-tuple-element.20) | data formatting | bytes 524288
  201.4 2.9 %copy.105 = f32[16,4096]{1,0:T(8,128)} copy(f32[16,4096]{0,1:T(8,128)} %get-tuple-element.21) | data formatting | bytes 524288
  (68 shorter events, 25.3 us)
Async XLA Ops:
  7.2 58.7 %copy-start = (bf16[96,128,128]{2,1,0:T(8,128)(2,1)S(1)}, bf16[96,128,128]{2,1,0:T(8,128)(2,1)}, u32[]{:S(2)}) copy-start(bf16[96,128,128]{2,1,0:T(8,128)(2,1)} %param.13) | copy-start | bytes 9437188
  12.6 41.8 %all-to-all-start = ((s32[8,1,2]{2,1,0:T(1,128)}), s32[8,1,2]{2,1,0:T(1,128)S(1)}, u32[]{:S(2)}, u32[]{:S(2)}) async-start(s32[8,1,2]{2,1,0:T(1,128)} %copy.88), calls=%async_computation | async-start | bytes 8192 | tf_op jit(solution)/shard_map/all_to_all | solution.py:61
  37.6 15.4 %copy-start.8 = (s32[96]{0:T(128)S(1)}, s32[96]{0:T(128)}, u32[]{:S(2)}) copy-start(s32[96]{0:T(128)} %param.12) | copy-start | bytes 1156
  49.9 2.9 %copy-start.1 = (bf16[32,4096]{1,0:T(8,128)(2,1)}, bf16[32,4096]{1,0:T(8,128)(2,1)S(1)}, u32[]{:S(2)}) copy-start(bf16[32,4096]{1,0:T(8,128)(2,1)S(1)} %all_gather.6) | copy-start | bytes 786436
  50.0 13.3 %collective-permute-start = (bf16[32,256]{1,0:T(8,128)(2,1)S(1)}, bf16[32,256]{1,0:T(8,128)(2,1)S(1)}, u32[]{:S(2)}, u32[]{:S(2)}) collective-permute-start(bf16[32,256]{1,0:T(8,128)(2,1)S(1)} %get-tuple-element.24), channel_id=1, source_target_pairs={{0,2},{2,4},{4,6},{6,8},{8,10},{10,12},{12,14},{1,3},{3,5},{5,7},{... | collective-permute-start | bytes 49160 | tf_op jit(solution)/shard_map/ppermute | solution.py:17
  51.6 11.7 %collective-permute-start.1 = (bf16[32,256]{1,0:T(8,128)(2,1)S(1)}, bf16[32,256]{1,0:T(8,128)(2,1)S(1)}, u32[]{:S(2)}, u32[]{:S(2)}) collective-permute-start(bf16[32,256]{1,0:T(8,128)(2,1)S(1)} %get-tuple-element.25), channel_id=1, source_target_pairs={{2,0},{4,2},{6,4},{8,6},{10,8},{12,10},{14,12},{3,1},{5,3},{7,5},{... | collective-permute-start | bytes 49160 | tf_op jit(solution)/shard_map/ppermute | solution.py:18
  53.0 1.5 copy-start.5
  55.9 14.3 %all-to-all-start.1 = ((bf16[32,8,2,128]{3,0,2,1:T(8,128)(2,1)}), bf16[32,8,2,128]{3,0,2,1:T(8,128)(2,1)}, u32[]{:S(2)}, u32[]{:S(2)}) async-start(bf16[32,8,2,128]{3,0,2,1:T(8,128)(2,1)} %bitcast.10), calls=%async_computation.1 | async-start | bytes 262144 | tf_op jit(solution)/shard_map/all_to_all | solution.py:71
  63.2 38.9 %reduce-scatter.7.cloned.1.call-start = ((), (), s32[]{:S(2)}) async-start(), calls=%async_computation.5 | async-start | bytes 786432 | tf_op jit(solution)/shard_map/reduce_scatter | solution.py:84
  102.1 21.5 %copy-start.3 = (f32[16,4096]{1,0:T(8,128)S(1)}, f32[16,4096]{1,0:T(8,128)}, u32[]{:S(2)}) copy-start(f32[16,4096]{1,0:T(8,128)} %reduce-scatter.7.cloned.1.call-done) | copy-start | bytes 786436
  129.3 2.6 %copy-start.2 = (bf16[32,4096]{1,0:T(8,128)(2,1)}, bf16[32,4096]{1,0:T(8,128)(2,1)S(1)}, u32[]{:S(2)}) copy-start(bf16[32,4096]{1,0:T(8,128)(2,1)S(1)} %all_gather.7) | copy-start | bytes 786436
  129.3 9.6 %collective-permute-start.2 = (bf16[32,256]{1,0:T(8,128)(2,1)S(1)}, bf16[32,256]{1,0:T(8,128)(2,1)S(1)}, u32[]{:S(2)}, u32[]{:S(2)}) collective-permute-start(bf16[32,256]{1,0:T(8,128)(2,1)S(1)} %get-tuple-element.22), channel_id=1, source_target_pairs={{0,2},{2,4},{4,6},{6,8},{8,10},{10,12},{12,14},{1,3},{3,5},{5,7},{... | collective-permute-start | bytes 49160 | tf_op jit(solution)/shard_map/ppermute | solution.py:17
  130.6 8.3 %collective-permute-start.3 = (bf16[32,256]{1,0:T(8,128)(2,1)S(1)}, bf16[32,256]{1,0:T(8,128)(2,1)S(1)}, u32[]{:S(2)}, u32[]{:S(2)}) collective-permute-start(bf16[32,256]{1,0:T(8,128)(2,1)S(1)} %get-tuple-element.23), channel_id=1, source_target_pairs={{2,0},{4,2},{6,4},{8,6},{10,8},{12,10},{14,12},{3,1},{5,3},{7,5},{... | collective-permute-start | bytes 49160 | tf_op jit(solution)/shard_map/ppermute | solution.py:18
  134.7 10.9 %all-to-all-start.2 = ((bf16[32,8,2,128]{3,0,2,1:T(8,128)(2,1)}), bf16[32,8,2,128]{3,0,2,1:T(8,128)(2,1)}, u32[]{:S(2)}, u32[]{:S(2)}) async-start(bf16[32,8,2,128]{3,0,2,1:T(8,128)(2,1)} %bitcast.22), calls=%async_computation.2 | async-start | bytes 262144 | tf_op jit(solution)/shard_map/all_to_all | solution.py:71
  138.7 37.9 %reduce-scatter.9.cloned.1.call-start = ((), (), s32[]{:S(2)}) async-start(), calls=%async_computation.6 | async-start | bytes 786432 | tf_op jit(solution)/shard_map/reduce_scatter | solution.py:84
  145.5 4.4 %copy-start.6 = (s32[46]{0:T(128)S(1)}, s32[46]{0:T(128)}, u32[]{:S(2)}) copy-start(s32[46]{0:T(128)} %param.14) | copy-start | bytes 556
  145.5 6.4 %copy-start.7 = (s32[96]{0:T(128)S(1)}, s32[96]{0:T(128)}, u32[]{:S(2)}) copy-start(s32[96]{0:T(128)} %param.11) | copy-start | bytes 1156
  158.6 17.9 %copy-start.4 = (f32[16,4096]{1,0:T(8,128)S(1)}, f32[16,4096]{1,0:T(8,128)}, u32[]{:S(2)}) copy-start(f32[16,4096]{1,0:T(8,128)} %reduce-scatter.7.cloned.1.call-done) | copy-start | bytes 786436
Sparse Core Ops, SparseCore 0:
  86.3 15.7 reduce-scatter.6
  161.8 14.7 reduce-scatter.8
where the time goes:
time: 212 us; the launch traced here: 211 us
  local copies, waits for them, and re-layouts  76.1 us (36%)
  waiting for transfers between devices  31.1 us (15%)
  blocking collectives  28.6 us (13%)
  matrix products  24.6 us (12%)
  starting transfers between devices  23.5 us (11%)
  between operations  14.3 us (7%)
  other arithmetic  13 us (6%)
    reduce_scatter x2, waiting for transfers between devices, operate(): lax.psum_scatter(placed.reshape(field.shape[0] * lax.axis_size('rhs'), pa...  30.8 us
    unnamed x24, local copies, waits for them, and re-layouts  17 us
    psum x1, blocking collectives, on_device(): totals = lax.psum(squares, 'panels')  16.3 us
    gather x1, local copies, waits for them, and re-layouts, on_device(): tree = jnp.take(incident, local_order, axis=1)  15.7 us
    scatter x1, local copies, waits for them, and re-layouts, on_device(): images = jnp.zeros_like(both).at[:, local_order].set(both)  12.3 us
    all_gather x2, blocking collectives, operate(): every = lax.all_gather(field, 'rhs', axis=0, tiled=True)  12.2 us
    all_to_all x2, starting transfers between devices, operate(): lax.all_to_all(served, 'panels', split_axis=1, concat_axis=1, tiled=True)  11.4 us
    dot_general x2, matrix products, operate(): jnp.einsum('ekj,hej->hek', near_blocks, near_input, preferred_element_typ...  8.07 us
  transfers between devices with their start and end apart: 9, of which 3 were waited for; matrix products, arithmetic and copies ran while one was open for 20% of the time, Pallas kernels for 0%

commit v1 on v0

v1 whole, which is shorter than its diff:
```python
import functools

import jax
import jax.numpy as jnp
from jax import lax
from jax.experimental import pallas as pl
from jax.experimental.pallas import tpu as pltpu
from jax.sharding import PartitionSpec as P

MESH = pl.DeviceIdType.MESH
REACH = 2
CAPACITY = 2
LAST = (((1,), (1,)), ((), ()))
CHUNKS = 4
ROWS = 16


def sort_list(rows_ref, count, clusters, meta, base, cnt, start, index_of):
    perm, index, keep, end = base, base + count, base + 2 * count, base + 3 * count

    def clear(c, _):
        cnt[c] = 0
        return 0

    lax.fori_loop(0, clusters + 1, clear, 0, unroll=True)

    def tally(e, _):
        r = rows_ref[e]
        cnt[r] = cnt[r] + 1
        return 0

    lax.fori_loop(0, count, tally, 0, unroll=2)

    def prefix(c, run):
        n = cnt[c]
        cnt[c] = run
        start[c] = run
        meta[end + c] = jnp.where(n > 0, run + n - 1, count)
        return run + n

    lax.fori_loop(0, clusters + 1, prefix, 0, unroll=3)

    def place(e, _):
        r = rows_ref[e]
        pos = cnt[r]
        cnt[r] = pos + 1
        meta[perm + pos] = e
        meta[index + pos] = index_of(e)
        meta[keep + pos] = jnp.where(pos == start[r], 0, 1)
        return 0

    lax.fori_loop(0, count, place, 0, unroll=2)
    return end + clusters + 1


def prepare(clusters, owners, near_rows, near_sources, far_rows, far_sources, meta, asks, cnt, start, seen):
    owner = lax.axis_index("panels")
    near, far = near_rows.shape[0], far_rows.shape[0]
    first = owner * clusters - REACH

    def near_index(e):
        return near_sources[e] - first

    base = sort_list(near_rows, near, clusters, meta, 0, cnt, start, near_index)

    def clear(q, _):
        seen[q] = 0
        return 0

    lax.fori_loop(0, owners, clear, 0, unroll=True)

    def far_index(e):
        source = far_sources[e]
        target = source // clusters
        within = source - target * clusters
        slot = seen[target]
        seen[target] = slot + 1
        asks[target, 0, slot] = within
        return jnp.where(
            target == owner, within + REACH, clusters + 2 * REACH + CAPACITY * target + slot
        )

    sort_list(far_rows, far, clusters, meta, base, cnt, start, far_index)


def permute(source, index_ref, clusters, emit):
    def group(t, _):
        index = jnp.broadcast_to(index_ref[pl.ds(t, 1), :], (ROWS, 128))
        low, high = index & 127, index >> 7
        tile = jnp.zeros((ROWS, 128), jnp.float32)
        for s in range(clusters):
            moved = jnp.take_along_axis(source[s], low, axis=1, mode="promise_in_bounds")
            tile = jnp.where(high == s, moved, tile)
        emit(t, tile)
        return 0

    lax.fori_loop(0, clusters, group, 0)


def kernel(
    clusters,
    owners,
    shares,
    near,
    far,
    incident,
    order,
    asks,
    meta,
    near_hbm,
    far_left,
    far_right,
    first_image,
    second_image,
    blocks,
    values,
    local,
    inverse,
    own_a,
    own_b,
    table_a,
    table_b,
    stage_a,
    stage_b,
    near_sums,
    far_sums,
    send_a,
    send_b,
    recv_a,
    recv_b,
    asked_v,
    asked_s,
    squares,
    all_squares,
    load_sem,
    asked_sem,
    ask_send,
    ask_recv,
    seg_send,
    seg_recv,
    halo_send,
    halo_recv,
    half_send,
    half_recv,
    sum_send,
    sum_recv,
    sq_send,
    sq_recv,
):
    p = lax.axis_index("panels")
    r = lax.axis_index("rhs")
    span = clusters // CHUNKS
    slots = clusters + 2 * REACH

    load = pltpu.make_async_copy(near_hbm, blocks, load_sem)
    load.start()

    def peers(body):
        def step(j, _):
            q = lax.rem(p + j, owners)
            for s in range(shares):
                body(q, s)
            return 0

        lax.fori_loop(1, owners, step, 0)

    def others(body):
        for j in range(1, shares):
            body(lax.rem(r + j, shares))

    barrier = pltpu.get_barrier_semaphore()

    def greet(q, s):
        pl.semaphore_signal(
            barrier, inc=1, device_id={"panels": q, "rhs": s}, device_id_type=MESH
        )

    peers(greet)
    others(lambda s: greet(p, s))

    asked_v[p] = jnp.zeros_like(asked_v[p])
    for s in range(clusters):
        values[s] = incident[:, s * 128 : (s + 1) * 128].astype(jnp.float32)
    local[...] = order[...] - p * (clusters * 128)
    near_sums[near] = jnp.zeros_like(near_sums[near])
    far_sums[far] = jnp.zeros_like(far_sums[far])

    pl.semaphore_wait(barrier, shares * owners - 1)

    def ask_copy(q, s, src_owner, src_rhs):
        return pltpu.make_async_remote_copy(
            src_ref=asks.at[q],
            dst_ref=asked_v.at[src_owner, src_rhs],
            send_sem=ask_send.at[q, s],
            recv_sem=ask_recv.at[src_owner, src_rhs],
            device_id={"panels": q, "rhs": s},
            device_id_type=MESH,
        )

    peers(lambda q, s: ask_copy(q, s, p, r).start())

    def half_copy(phase, own, table, k, s, src_rhs):
        return pltpu.make_async_remote_copy(
            src_ref=own.at[pl.ds(k * span, span)],
            dst_ref=table.at[pl.ds(REACH + k * span, span), src_rhs],
            send_sem=half_send.at[phase, k, s],
            recv_sem=half_recv.at[phase, k, src_rhs],
            device_id={"panels": p, "rhs": s},
            device_id_type=MESH,
        )

    def seg_copy(phase, stage, table, q, s, src_owner, src_rhs):
        return pltpu.make_async_remote_copy(
            src_ref=stage.at[q, s],
            dst_ref=table.at[pl.ds(slots + CAPACITY * src_owner, CAPACITY), src_rhs],
            send_sem=seg_send.at[phase, q, s],
            recv_sem=seg_recv.at[phase, src_owner, src_rhs],
            device_id={"panels": q, "rhs": s},
            device_id_type=MESH,
        )

    def halo_copy(phase, own, table, up, q, s, src_rhs):
        src, dst = (clusters - REACH, 0) if up else (0, clusters + REACH)
        side = 0 if up else 1
        return pltpu.make_async_remote_copy(
            src_ref=own.at[pl.ds(src, REACH)],
            dst_ref=table.at[pl.ds(dst, REACH), src_rhs],
            send_sem=halo_send.at[phase, side, s],
            recv_sem=halo_recv.at[phase, side, src_rhs],
            device_id={"panels": q, "rhs": s},
            device_id_type=MESH,
        )

    has_next, has_last = p < owners - 1, p > 0

    def halos(phase, own, table, act):
        @pl.when(has_next)
        def _():
            for s in range(shares):
                act(halo_copy(phase, own, table, True, p + 1, s, r), True)

        @pl.when(has_last)
        def _():
            for s in range(shares):
                act(halo_copy(phase, own, table, False, p - 1, s, r), False)

    def spread(phase, own, table, stage):
        halos(phase, own, table, lambda copy, _: copy.start())

        def serve(q, s):
            for k in range(CAPACITY):
                stage[q, s, k] = own[asked_s[q, s, 0, k]]
            seg_copy(phase, stage, table, q, s, p, r).start()

        peers(serve)

    def gathered(phase, own, table, stage):
        for k in range(CHUNKS):
            others(lambda s: half_copy(phase, own, table, k, s, s).wait_recv())

        @pl.when(has_last)
        def _():
            for s in range(shares):
                halo_copy(phase, own, table, True, p, s, s).wait_recv()

        @pl.when(has_next)
        def _():
            for s in range(shares):
                halo_copy(phase, own, table, False, p, s, s).wait_recv()

        peers(lambda q, s: seg_copy(phase, stage, table, q, s, q, s).wait_recv())

    def sent(phase, own, table, stage):
        for k in range(CHUNKS):
            others(lambda s: half_copy(phase, own, table, k, s, r).wait_send())
        halos(phase, own, table, lambda copy, _: copy.wait_send())
        peers(lambda q, s: seg_copy(phase, stage, table, q, s, p, r).wait_send())

    base = 3 * near + clusters + 1

    def apply(table):
        def near_step(i, acc):
            segment = table[meta[near + i]].reshape(shares * ROWS, 128)
            block = blocks[meta[i]]
            term = lax.dot_general(segment, block, LAST, preferred_element_type=jnp.float32)
            acc = acc * meta[2 * near + i].astype(jnp.float32) + term
            near_sums[i] = acc.reshape(shares, ROWS, 128)
            return acc

        def far_step(i, acc):
            segment = table[meta[base + far + i]].reshape(shares * ROWS, 128)
            entry = meta[base + i]
            coefficients = lax.dot_general(
                segment, far_right[entry], LAST, preferred_element_type=jnp.float32
            ).astype(jnp.bfloat16)
            term = jnp.dot(coefficients, far_left[entry], preferred_element_type=jnp.float32)
            acc = acc * meta[base + 2 * far + i].astype(jnp.float32) + term
            far_sums[i] = acc.reshape(shares, ROWS, 128)
            return acc

        zero = jnp.zeros((shares * ROWS, 128), jnp.float32)
        lax.fori_loop(0, far, far_step, zero, unroll=4 if shares > 2 else far)
        lax.fori_loop(0, near, near_step, zero, unroll=16)

    def part(c, s):
        return (
            near_sums[meta[3 * near + c], s] + far_sums[meta[base + 3 * far + c], s]
        )

    def sum_copy(phase, send, recv, k, s, src_rhs):
        return pltpu.make_async_remote_copy(
            src_ref=send.at[s, pl.ds(k * span, span)],
            dst_ref=recv.at[src_rhs, pl.ds(k * span, span)],
            send_sem=sum_send.at[phase, k, s],
            recv_sem=sum_recv.at[phase, k, src_rhs],
            device_id={"panels": p, "rhs": s},
            device_id_type=MESH,
        )

    def reduce(phase, send, recv, take, after):
        def give(k, s):
            for c in range(k * span, (k + 1) * span):
                send[s, c] = part(c, s)
            sum_copy(phase, send, recv, k, s, r).start()

        for k in range(CHUNKS):
            others(lambda s: give(k, s))
        for k in range(CHUNKS):
            others(lambda s: sum_copy(phase, send, recv, k, s, s).wait_recv())
            for c in range(k * span, (k + 1) * span):
                tile = part(c, r)
                for j in range(1, shares):
                    tile = tile + recv[lax.rem(r + j, shares), c]
                take(c, tile)
            after(k)

    def tree_tile(t, tile):
        tile = tile.astype(jnp.bfloat16)
        own_a[t] = tile
        table_a[REACH + t, r] = tile

    permute(values, local, clusters, tree_tile)
    for k in range(CHUNKS):
        others(lambda s: half_copy(0, own_a, table_a, k, s, r).start())
    peers(lambda q, s: ask_copy(q, s, q, s).wait_recv())
    to_scalar = pltpu.make_async_copy(asked_v, asked_s, asked_sem)
    to_scalar.start()
    to_scalar.wait()
    spread(0, own_a, table_a, stage_a)

    digits = jnp.zeros((2 * clusters, 128), jnp.float32)
    lane = lax.broadcasted_iota(jnp.int32, (1, 128), 1)
    for s in range(clusters):
        row = local[s : s + 1, :]
        groups = lax.broadcasted_iota(jnp.int32, (clusters, 128), 0) == (row >> 7)
        position = lane + s * 128
        top = jnp.where(groups, (position >> 6).astype(jnp.float32), 0.0)
        bottom = jnp.where(groups, (position & 63).astype(jnp.float32), 0.0)
        left = jnp.concatenate([top, bottom], axis=0).astype(jnp.bfloat16)
        hot = lax.broadcasted_iota(jnp.int32, (128, 128), 0) == (row & 127)
        hot = jnp.where(hot, 1.0, 0.0).astype(jnp.bfloat16)
        digits = digits + lax.dot_general(left, hot, LAST, preferred_element_type=jnp.float32)
    inverse[...] = (digits[:clusters] * 64.0 + digits[clusters:]).astype(jnp.int32)

    load.wait()
    gathered(0, own_a, table_a, stage_a)
    apply(table_a)

    squares[...] = jnp.zeros_like(squares)

    def first_tile(c, tile):
        values[c] = tile
        squares[...] += tile * tile
        tile = tile.astype(jnp.bfloat16)
        own_b[c] = tile
        table_b[REACH + c, r] = tile

    def share(k):
        others(lambda s: half_copy(1, own_b, table_b, k, s, r).start())

    reduce(0, send_a, recv_a, first_tile, share)
    spread(1, own_b, table_b, stage_b)

    def sq_copy(q, src_owner):
        return pltpu.make_async_remote_copy(
            src_ref=squares,
            dst_ref=all_squares.at[src_owner],
            send_sem=sq_send.at[q],
            recv_sem=sq_recv.at[src_owner],
            device_id={"panels": q, "rhs": r},
            device_id_type=MESH,
        )

    def same(body):
        def step(j, _):
            body(lax.rem(p + j, owners))
            return 0

        lax.fori_loop(1, owners, step, 0)

    same(lambda q: sq_copy(q, p).start())
    all_squares[p] = squares[...]

    def first_out(t, tile):
        first_image[:, pl.ds(pl.multiple_of(t * 128, 128), 128)] = tile

    permute(values, inverse, clusters, first_out)

    gathered(1, own_b, table_b, stage_b)
    apply(table_b)
    same(lambda q: sq_copy(q, q).wait_recv())
    total = lax.fori_loop(
        0, owners, lambda q, acc: acc + all_squares[q], jnp.zeros((ROWS, 128), jnp.float32)
    )
    total = jnp.sum(total, axis=1, keepdims=True)
    scale = lax.rsqrt(total / (clusters * 128 * owners) + 1e-06)

    def second_tile(c, tile):
        values[c] = tile * scale

    reduce(1, send_b, recv_b, second_tile, lambda k: None)

    def second_out(t, tile):
        second_image[:, pl.ds(pl.multiple_of(t * 128, 128), 128)] = tile

    permute(values, inverse, clusters, second_out)

    peers(lambda q, s: ask_copy(q, s, p, r).wait_send())
    sent(0, own_a, table_a, stage_a)
    sent(1, own_b, table_b, stage_b)
    for k in range(CHUNKS):
        others(lambda s: sum_copy(0, send_a, recv_a, k, s, r).wait_send())
        others(lambda s: sum_copy(1, send_b, recv_b, k, s, r).wait_send())
    same(lambda q: sq_copy(q, p).wait_send())


def on_device(
    owners,
    shares,
    incident,
    tree_order,
    near_rows,
    near_sources,
    near_blocks,
    far_rows,
    far_sources,
    far_left,
    far_right,
):
    headings, panels = incident.shape
    incident = jnp.pad(incident, ((0, ROWS - headings), (0, 0)))
    near, block = near_blocks.shape[:2]
    far, rank = far_left.shape[:2]
    clusters = panels // block
    slots = clusters + 2 * REACH + CAPACITY * owners
    smem = pl.BlockSpec(memory_space=pltpu.SMEM)
    vmem = pl.BlockSpec(memory_space=pltpu.VMEM)
    meta_size = 3 * (near + far) + 2 * (clusters + 1)
    meta, asks = pl.pallas_call(
        functools.partial(prepare, clusters, owners),
        out_shape=(
            jax.ShapeDtypeStruct((meta_size,), jnp.int32),
            jax.ShapeDtypeStruct((owners, 1, 128), jnp.int32),
        ),
        in_specs=[smem] * 4,
        out_specs=(smem, smem),
        scratch_shapes=[
            pltpu.SMEM((clusters + 1,), jnp.int32),
            pltpu.SMEM((clusters + 1,), jnp.int32),
            pltpu.SMEM((owners,), jnp.int32),
        ],
    )(near_rows, near_sources, far_rows, far_sources)
    bf, f32 = jnp.bfloat16, jnp.float32
    dma = pltpu.SemaphoreType.DMA
    image = jax.ShapeDtypeStruct((ROWS, panels), f32)
    first, second = pl.pallas_call(
        functools.partial(kernel, clusters, owners, shares, near, far),
        out_shape=(image, image),
        in_specs=[vmem, vmem, vmem, smem, pl.BlockSpec(memory_space=pl.ANY), vmem, vmem],
        out_specs=(vmem, vmem),
        scratch_shapes=[
            pltpu.VMEM((near, block, block), bf),
            pltpu.VMEM((clusters, ROWS, block), f32),
            pltpu.VMEM((clusters, block), jnp.int32),
            pltpu.VMEM((clusters, block), jnp.int32),
            pltpu.VMEM((clusters, ROWS, block), bf),
            pltpu.VMEM((clusters, ROWS, block), bf),
            pltpu.VMEM((slots, shares, ROWS, block), bf),
            pltpu.VMEM((slots, shares, ROWS, block), bf),
            pltpu.VMEM((owners, shares, CAPACITY, ROWS, block), bf),
            pltpu.VMEM((owners, shares, CAPACITY, ROWS, block), bf),
            pltpu.VMEM((near + 1, shares, ROWS, block), f32),
            pltpu.VMEM((far + 1, shares, ROWS, block), f32),
            pltpu.VMEM((shares, clusters, ROWS, block), f32),
            pltpu.VMEM((shares, clusters, ROWS, block), f32),
            pltpu.VMEM((shares, clusters, ROWS, block), f32),
            pltpu.VMEM((shares, clusters, ROWS, block), f32),
            pltpu.VMEM((owners, shares, 1, 128), jnp.int32),
            pltpu.SMEM((owners, shares, 1, 128), jnp.int32),
            pltpu.VMEM((ROWS, block), f32),
            pltpu.VMEM((owners, ROWS, block), f32),
            dma,
            dma,
            dma((owners, shares)),
            dma((owners, shares)),
            dma((2, owners, shares)),
            dma((2, owners, shares)),
            dma((2, 2, shares)),
            dma((2, 2, shares)),
            dma((2, CHUNKS, shares)),
            dma((2, CHUNKS, shares)),
            dma((2, CHUNKS, shares)),
            dma((2, CHUNKS, shares)),
            dma((owners,)),
            dma((owners,)),
        ],
        compiler_params=pltpu.CompilerParams(
            collective_id=0, has_side_effects=True, vmem_limit_bytes=56 * 2**20
        ),
    )(
        incident,
        tree_order.reshape(clusters, block),
        asks,
        meta,
        near_blocks,
        far_left,
        far_right,
    )
    return first[:headings], second[:headings]


def solution(mesh):
    lists = ("groups", "panels", "rhs")
    in_specs = (
        P("rhs", ("groups", "panels")),
        P(("groups", "panels")),
        P(lists),
        P(lists),
        P(lists, None, None),
        P(lists),
        P(lists),
        P(lists, None, None),
        P(lists, None, None),
    )
    out_specs = (P("rhs", ("groups", "panels")), P("rhs", ("groups", "panels")))
    return jax.shard_map(
        functools.partial(on_device, mesh.shape["panels"], mesh.shape["rhs"]),
        mesh=mesh,
        in_specs=in_specs,
        out_specs=out_specs,
        check_vma=False,
    )
```

time: 212 us -> 63.8 us (0.30)
  local copies, waits for them, and re-layouts: 76.1 us -> 3.34 us
  Pallas kernels: 0 us -> 59.6 us
  waiting for transfers between devices: 31.1 us -> 0 us
  blocking collectives: 28.6 us -> 0 us
  matrix products: 24.6 us -> 0 us
  starting transfers between devices: 23.5 us -> 0 us
  between operations: 14.3 us -> 0.65 us
  other arithmetic: 13 us -> 0 us
    pallas_call x0 -> x2, Pallas kernels: none -> 59.6 us  [the longest x1 55.4 us: on_device(): pl.pallas_call(functools.partial(kernel, clusters, owners, shares, near,...]
    reduce_scatter x2 -> x0, waiting for transfers between devices: 30.8 us -> none  [operate(): lax.psum_scatter(placed.reshape(field.shape[0] * lax.axis_size('rhs'), pa...]
    gather x9 -> x0, local copies, waits for them, and re-layouts: 27.6 us -> none  [the longest x1 15.7 us: on_device(): tree = jnp.take(incident, local_order, axis=1)]
    dot_general x8 -> x0, matrix products: 24.6 us -> none  [the longest x2 8.07 us: operate(): jnp.einsum('ekj,hej->hek', near_blocks, near_input, preferred_element_typ...]
    all_to_all x3 -> x0, starting transfers between devices: 17.7 us -> none  [the longest x2 11.4 us: operate(): lax.all_to_all(served, 'panels', split_axis=1, concat_axis=1, tiled=True)]
    psum x1 -> x0, blocking collectives: 16.3 us -> none  [on_device(): totals = lax.psum(squares, 'panels')]
    scatter x2 -> x0, local copies, waits for them, and re-layouts: 15.1 us -> none  [the longest x1 12.3 us: on_device(): images = jnp.zeros_like(both).at[:, local_order].set(both)]
    unnamed x24 -> x2, local copies, waits for them, and re-layouts: 17 us -> 3.34 us
  transfers between devices with their start and end apart: 9 -> 0, of which waited for: 3 -> 0; matrix products, arithmetic and copies ran while one was open for 20% -> 0% of each run, Pallas kernels for 0% -> 0%
where the time goes in v1:
time: 63.8 us; the launch traced here: 63.5 us
  Pallas kernels  59.6 us (93%)
  local copies, waits for them, and re-layouts  3.34 us (5%)
  between operations  0.65 us (1%)
    pallas_call x1, Pallas kernels, on_device(): pl.pallas_call(functools.partial(kernel, clusters, owners, shares, near,...  55.4 us
    pallas_call x1, Pallas kernels, on_device(): pl.pallas_call(functools.partial(prepare, clusters, owners), out_shape=(j...  4.17 us
    unnamed x2, local copies, waits for them, and re-layouts  3.34 us

profile of v1, /device:TPU:0, one launch (start us, length us, event | category | flops | bytes accessed | tf_op | source)
XLA Modules:
  0.0 63.5 jit_solution(4478316763905566124)
XLA Ops:
  0.6 4.2 %shard_map.104 = (s32[492]{0:T(512)}, s32[8,1,128]{2,1,0:T(1,128)}) custom-call(s32[96]{0:T(128)} %near_rows.1, s32[96]{0:T(128)} %near_sources.1, s32[46]{0:T(128)} %far_rows.1, s32[46]{0:T(128)} %far_sources.1), custom_call_target="tpu_custom_call" | custom-call | tf_op jit(solution)/shard_map/pallas_call | solution.py:459
  4.8 55.4 %shard_map.105 = (f32[16,4096]{1,0:T(8,128)}, f32[16,4096]{1,0:T(8,128)}) custom-call(bf16[16,4096]{1,0:T(8,128)(2,1)} %incident.1, s32[32,128]{1,0:T(8,128)} %bitcast.1, s32[8,1,128]{2,1,0:T(1,128)} %get-tuple-element.4.asks, s32[492]{0:T(512)} %get-tuple-element.5.meta, bf16[96,128,128]{2,1,0:T(8,128)(2,1)} %near_hbm.1, bf16[46,16,128]{2,1,0:T(8,128)(2,1)} %far_left.1, ...), custom_call_target="tpu_custom_call" | custom-call | tf_op jit(solution)/shard_map/pallas_call | solution.py:476
  60.2 1.7 %copy.13 = f32[16,4096]{1,0:T(8,128)} copy(f32[16,4096]{1,0:T(8,128)} %get-tuple-element.8) | data formatting | bytes 524288
  61.9 1.7 %copy.14 = f32[16,4096]{1,0:T(8,128)} copy(f32[16,4096]{1,0:T(8,128)} %get-tuple-element.9) | data formatting | bytes 524288

commit v2 on v1

--- a/solution.py
+++ b/solution.py
@@ -84,17 +84,14 @@
 
 
 def permute(source, index_ref, clusters, emit):
-    def group(t, _):
-        index = jnp.broadcast_to(index_ref[pl.ds(t, 1), :], (ROWS, 128))
+    for t in range(clusters):
+        index = jnp.broadcast_to(index_ref[t : t + 1, :], (ROWS, 128))
         low, high = index & 127, index >> 7
         tile = jnp.zeros((ROWS, 128), jnp.float32)
         for s in range(clusters):
             moved = jnp.take_along_axis(source[s], low, axis=1, mode="promise_in_bounds")
             tile = jnp.where(high == s, moved, tile)
         emit(t, tile)
-        return 0
-
-    lax.fori_loop(0, clusters, group, 0)
 
 
 def kernel(
@@ -111,11 +108,11 @@
     far_left,
     far_right,
     first_image,
-    second_image,
+    second_tree,
+    inverse,
     blocks,
     values,
     local,
-    inverse,
     own_a,
     own_b,
     table_a,
@@ -136,12 +133,8 @@
     asked_sem,
     ask_send,
     ask_recv,
-    seg_send,
-    seg_recv,
-    halo_send,
-    halo_recv,
-    half_send,
-    half_recv,
+    out_sem,
+    in_sem,
     sum_send,
     sum_recv,
     sq_send,
@@ -191,8 +184,8 @@
         return pltpu.make_async_remote_copy(
             src_ref=asks.at[q],
             dst_ref=asked_v.at[src_owner, src_rhs],
-            send_sem=ask_send.at[q, s],
-            recv_sem=ask_recv.at[src_owner, src_rhs],
+            send_sem=ask_send,
+            recv_sem=ask_recv,
             device_id={"panels": q, "rhs": s},
             device_id_type=MESH,
         )
@@ -203,8 +196,8 @@
         return pltpu.make_async_remote_copy(
             src_ref=own.at[pl.ds(k * span, span)],
             dst_ref=table.at[pl.ds(REACH + k * span, span), src_rhs],
-            send_sem=half_send.at[phase, k, s],
-            recv_sem=half_recv.at[phase, k, src_rhs],
+            send_sem=out_sem.at[phase],
+            recv_sem=in_sem.at[phase],
             device_id={"panels": p, "rhs": s},
             device_id_type=MESH,
         )
@@ -213,39 +206,27 @@
         return pltpu.make_async_remote_copy(
             src_ref=stage.at[q, s],
             dst_ref=table.at[pl.ds(slots + CAPACITY * src_owner, CAPACITY), src_rhs],
-            send_sem=seg_send.at[phase, q, s],
-            recv_sem=seg_recv.at[phase, src_owner, src_rhs],
+            send_sem=out_sem.at[phase],
+            recv_sem=in_sem.at[phase],
             device_id={"panels": q, "rhs": s},
             device_id_type=MESH,
         )
 
     def halo_copy(phase, own, table, up, q, s, src_rhs):
         src, dst = (clusters - REACH, 0) if up else (0, clusters + REACH)
-        side = 0 if up else 1
         return pltpu.make_async_remote_copy(
             src_ref=own.at[pl.ds(src, REACH)],
             dst_ref=table.at[pl.ds(dst, REACH), src_rhs],
-            send_sem=halo_send.at[phase, side, s],
-            recv_sem=halo_recv.at[phase, side, src_rhs],
+            send_sem=out_sem.at[phase],
+            recv_sem=in_sem.at[phase],
             device_id={"panels": q, "rhs": s},
             device_id_type=MESH,
         )
 
-    has_next, has_last = p < owners - 1, p > 0
-
-    def halos(phase, own, table, act):
-        @pl.when(has_next)
-        def _():
-            for s in range(shares):
-                act(halo_copy(phase, own, table, True, p + 1, s, r), True)
-
-        @pl.when(has_last)
-        def _():
-            for s in range(shares):
-                act(halo_copy(phase, own, table, False, p - 1, s, r), False)
-
     def spread(phase, own, table, stage):
-        halos(phase, own, table, lambda copy, _: copy.start())
+        for s in range(shares):
+            halo_copy(phase, own, table, True, lax.rem(p + 1, owners), s, r).start()
+            halo_copy(phase, own, table, False, lax.rem(p + owners - 1, owners), s, r).start()
 
         def serve(q, s):
             for k in range(CAPACITY):
@@ -254,39 +235,17 @@
 
         peers(serve)
 
-    def gathered(phase, own, table, stage):
-        for k in range(CHUNKS):
-            others(lambda s: half_copy(phase, own, table, k, s, s).wait_recv())
-
-        @pl.when(has_last)
-        def _():
-            for s in range(shares):
-                halo_copy(phase, own, table, True, p, s, s).wait_recv()
-
-        @pl.when(has_next)
-        def _():
-            for s in range(shares):
-                halo_copy(phase, own, table, False, p, s, s).wait_recv()
-
-        peers(lambda q, s: seg_copy(phase, stage, table, q, s, q, s).wait_recv())
-
-    def sent(phase, own, table, stage):
-        for k in range(CHUNKS):
-            others(lambda s: half_copy(phase, own, table, k, s, r).wait_send())
-        halos(phase, own, table, lambda copy, _: copy.wait_send())
-        peers(lambda q, s: seg_copy(phase, stage, table, q, s, p, r).wait_send())
+    moved = (shares - 1) * clusters // shares + (owners - 1) * CAPACITY + 2 * REACH
+
+    def wait_bytes(view, sem):
+        pltpu.make_async_copy(view, view, sem).wait()
+
+    def gathered(phase, table):
+        wait_bytes(table.at[pl.ds(0, moved)], in_sem.at[phase])
 
     base = 3 * near + clusters + 1
 
     def apply(table):
-        def near_step(i, acc):
-            segment = table[meta[near + i]].reshape(shares * ROWS, 128)
-            block = blocks[meta[i]]
-            term = lax.dot_general(segment, block, LAST, preferred_element_type=jnp.float32)
-            acc = acc * meta[2 * near + i].astype(jnp.float32) + term
-            near_sums[i] = acc.reshape(shares, ROWS, 128)
-            return acc
-
         def far_step(i, acc):
             segment = table[meta[base + far + i]].reshape(shares * ROWS, 128)
             entry = meta[base + i]
@@ -298,9 +257,29 @@
             far_sums[i] = acc.reshape(shares, ROWS, 128)
             return acc
 
-        zero = jnp.zeros((shares * ROWS, 128), jnp.float32)
-        lax.fori_loop(0, far, far_step, zero, unroll=4 if shares > 2 else far)
-        lax.fori_loop(0, near, near_step, zero, unroll=16)
+        rows = shares * ROWS
+        group = 2 if near % 2 == 0 else 1
+
+        def near_step(g, acc):
+            places = [g * group + k for k in range(group)]
+            segments = [table[meta[near + i]].reshape(rows, 128) for i in places]
+            weights = [blocks[meta[i]] for i in places]
+            terms = lax.dot_general(
+                jnp.concatenate(segments, axis=0),
+                jnp.concatenate(weights, axis=0),
+                LAST,
+                preferred_element_type=jnp.float32,
+            )
+            for k, i in enumerate(places):
+                term = terms[k * rows : (k + 1) * rows, k * 128 : (k + 1) * 128]
+                acc = acc * meta[2 * near + i].astype(jnp.float32) + term
+                near_sums[i] = acc.reshape(shares, ROWS, 128)
+            return acc
+
+        zero = jnp.zeros((rows, 128), jnp.float32)
+        steps = near // group
+        lax.fori_loop(0, far, far_step, zero, unroll=far if shares <= 2 else 2)
+        lax.fori_loop(0, steps, near_step, zero, unroll=steps if shares <= 2 else 2)
 
     def part(c, s):
         return (
@@ -311,7 +290,7 @@
         return pltpu.make_async_remote_copy(
             src_ref=send.at[s, pl.ds(k * span, span)],
             dst_ref=recv.at[src_rhs, pl.ds(k * span, span)],
-            send_sem=sum_send.at[phase, k, s],
+            send_sem=sum_send.at[phase],
             recv_sem=sum_recv.at[phase, k, src_rhs],
             device_id={"panels": p, "rhs": s},
             device_id_type=MESH,
@@ -320,7 +299,7 @@
     def reduce(phase, send, recv, take, after):
         def give(k, s):
             for c in range(k * span, (k + 1) * span):
-                send[s, c] = part(c, s)
+                send[s, c] = part(c, s).astype(jnp.bfloat16)
             sum_copy(phase, send, recv, k, s, r).start()
 
         for k in range(CHUNKS):
@@ -342,7 +321,7 @@
     permute(values, local, clusters, tree_tile)
     for k in range(CHUNKS):
         others(lambda s: half_copy(0, own_a, table_a, k, s, r).start())
-    peers(lambda q, s: ask_copy(q, s, q, s).wait_recv())
+    wait_bytes(asked_v.at[pl.ds(0, owners - 1)], ask_recv)
     to_scalar = pltpu.make_async_copy(asked_v, asked_s, asked_sem)
     to_scalar.start()
     to_scalar.wait()
@@ -363,7 +342,7 @@
     inverse[...] = (digits[:clusters] * 64.0 + digits[clusters:]).astype(jnp.int32)
 
     load.wait()
-    gathered(0, own_a, table_a, stage_a)
+    gathered(0, table_a)
     apply(table_a)
 
     squares[...] = jnp.zeros_like(squares)
@@ -385,8 +364,8 @@
         return pltpu.make_async_remote_copy(
             src_ref=squares,
             dst_ref=all_squares.at[src_owner],
-            send_sem=sq_send.at[q],
-            recv_sem=sq_recv.at[src_owner],
+            send_sem=sq_send,
+            recv_sem=sq_recv,
             device_id={"panels": q, "rhs": r},
             device_id_type=MESH,
         )
@@ -402,13 +381,13 @@
     all_squares[p] = squares[...]
 
     def first_out(t, tile):
-        first_image[:, pl.ds(pl.multiple_of(t * 128, 128), 128)] = tile
+        first_image[:, t * 128 : (t + 1) * 128] = tile
 
     permute(values, inverse, clusters, first_out)
 
-    gathered(1, own_b, table_b, stage_b)
+    gathered(1, table_b)
     apply(table_b)
-    same(lambda q: sq_copy(q, q).wait_recv())
+    wait_bytes(all_squares.at[pl.ds(0, owners - 1)], sq_recv)
     total = lax.fori_loop(
         0, owners, lambda q, acc: acc + all_squares[q], jnp.zeros((ROWS, 128), jnp.float32)
     )
@@ -416,22 +395,27 @@
     scale = lax.rsqrt(total / (clusters * 128 * owners) + 1e-06)
 
     def second_tile(c, tile):
-        values[c] = tile * scale
+        second_tree[c] = tile * scale
 
     reduce(1, send_b, recv_b, second_tile, lambda k: None)
 
-    def second_out(t, tile):
-        second_image[:, pl.ds(pl.multiple_of(t * 128, 128), 128)] = tile
-
-    permute(values, inverse, clusters, second_out)
-
-    peers(lambda q, s: ask_copy(q, s, p, r).wait_send())
-    sent(0, own_a, table_a, stage_a)
-    sent(1, own_b, table_b, stage_b)
-    for k in range(CHUNKS):
-        others(lambda s: sum_copy(0, send_a, recv_a, k, s, r).wait_send())
-        others(lambda s: sum_copy(1, send_b, recv_b, k, s, r).wait_send())
-    same(lambda q: sq_copy(q, p).wait_send())
+    wait_bytes(asked_v.at[pl.ds(0, owners - 1)], ask_send)
+    wait_bytes(table_a.at[pl.ds(0, moved)], out_sem.at[0])
+    wait_bytes(table_b.at[pl.ds(0, moved)], out_sem.at[1])
+    wait_bytes(send_a.at[pl.ds(0, shares - 1)], sum_send.at[0])
+    wait_bytes(send_b.at[pl.ds(0, shares - 1)], sum_send.at[1])
+    wait_bytes(all_squares.at[pl.ds(0, owners - 1)], sq_send)
+
+
+def finish(clusters, first_tree, second_tree, inverse, first_image, second_image, sem):
+    copy = pltpu.make_async_copy(first_tree, first_image, sem)
+    copy.start()
+
+    def emit(t, tile):
+        second_image[:, t * 128 : (t + 1) * 128] = tile
+
+    permute(second_tree, inverse, clusters, emit)
+    copy.wait()
 
 
 def on_device(
@@ -473,15 +457,18 @@
     bf, f32 = jnp.bfloat16, jnp.float32
     dma = pltpu.SemaphoreType.DMA
     image = jax.ShapeDtypeStruct((ROWS, panels), f32)
-    first, second = pl.pallas_call(
+    first, second, inverse = pl.pallas_call(
         functools.partial(kernel, clusters, owners, shares, near, far),
-        out_shape=(image, image),
+        out_shape=(
+            image,
+            jax.ShapeDtypeStruct((clusters, ROWS, block), f32),
+            jax.ShapeDtypeStruct((clusters, block), jnp.int32),
+        ),
         in_specs=[vmem, vmem, vmem, smem, pl.BlockSpec(memory_space=pl.ANY), vmem, vmem],
-        out_specs=(vmem, vmem),
+        out_specs=(vmem, vmem, vmem),
         scratch_shapes=[
             pltpu.VMEM((near, block, block), bf),
             pltpu.VMEM((clusters, ROWS, block), f32),
-            pltpu.VMEM((clusters, block), jnp.int32),
             pltpu.VMEM((clusters, block), jnp.int32),
             pltpu.VMEM((clusters, ROWS, block), bf),
             pltpu.VMEM((clusters, ROWS, block), bf),
@@ -491,28 +478,24 @@
             pltpu.VMEM((owners, shares, CAPACITY, ROWS, block), bf),
             pltpu.VMEM((near + 1, shares, ROWS, block), f32),
             pltpu.VMEM((far + 1, shares, ROWS, block), f32),
-            pltpu.VMEM((shares, clusters, ROWS, block), f32),
-            pltpu.VMEM((shares, clusters, ROWS, block), f32),
-            pltpu.VMEM((shares, clusters, ROWS, block), f32),
-            pltpu.VMEM((shares, clusters, ROWS, block), f32),
+            pltpu.VMEM((shares, clusters, ROWS, block), bf),
+            pltpu.VMEM((shares, clusters, ROWS, block), bf),
+            pltpu.VMEM((shares, clusters, ROWS, block), bf),
+            pltpu.VMEM((shares, clusters, ROWS, block), bf),
             pltpu.VMEM((owners, shares, 1, 128), jnp.int32),
             pltpu.SMEM((owners, shares, 1, 128), jnp.int32),
             pltpu.VMEM((ROWS, block), f32),
             pltpu.VMEM((owners, ROWS, block), f32),
             dma,
             dma,
-            dma((owners, shares)),
-            dma((owners, shares)),
-            dma((2, owners, shares)),
-            dma((2, owners, shares)),
-            dma((2, 2, shares)),
-            dma((2, 2, shares)),
+            dma,
+            dma,
+            dma((2,)),
+            dma((2,)),
+            dma((2,)),
             dma((2, CHUNKS, shares)),
-            dma((2, CHUNKS, shares)),
-            dma((2, CHUNKS, shares)),
-            dma((2, CHUNKS, shares)),
-            dma((owners,)),
-            dma((owners,)),
+            dma,
+            dma,
         ],
         compiler_params=pltpu.CompilerParams(
             collective_id=0, has_side_effects=True, vmem_limit_bytes=56 * 2**20
@@ -526,6 +509,14 @@
         far_left,
         far_right,
     )
+    anywhere = pl.BlockSpec(memory_space=pl.ANY)
+    first, second = pl.pallas_call(
+        functools.partial(finish, clusters),
+        out_shape=(image, image),
+        in_specs=[anywhere, vmem, vmem],
+        out_specs=(anywhere, vmem),
+        scratch_shapes=[dma],
+    )(first, second, inverse)
     return first[:headings], second[:headings]
 
 

time: 63.8 us -> 56.7 us (0.89)
  Pallas kernels: 59.6 us -> 55.9 us
  local copies, waits for them, and re-layouts: 3.34 us -> 0 us
    pallas_call x1, Pallas kernels: 55.4 us -> 41 us  [on_device(): pl.pallas_call(functools.partial(kernel, clusters, owners, shares, near,...]
    pallas_call x0 -> x1, Pallas kernels: none -> 10.7 us  [on_device(): pl.pallas_call(functools.partial(finish, clusters), out_shape=(image, ima...]
    unnamed x2 -> x0, local copies, waits for them, and re-layouts: 3.34 us -> none
where the time goes in v2:
time: 56.7 us; the launch traced here: 56.6 us
  Pallas kernels  55.9 us (99%)
  between operations  0.65 us (1%)
    pallas_call x1, Pallas kernels, on_device(): pl.pallas_call(functools.partial(kernel, clusters, owners, shares, near,...  41 us
    pallas_call x1, Pallas kernels, on_device(): pl.pallas_call(functools.partial(finish, clusters), out_shape=(image, ima...  10.7 us
    pallas_call x1, Pallas kernels, on_device(): pl.pallas_call(functools.partial(prepare, clusters, owners), out_shape=(j...  4.17 us

profile of v2, /device:TPU:0, one launch (start us, length us, event | category | flops | bytes accessed | tf_op | source)
XLA Modules:
  0.0 56.6 jit_solution(2140651164376585189)
XLA Ops:
  0.6 4.2 %shard_map.104 = (s32[492]{0:T(512)}, s32[8,1,128]{2,1,0:T(1,128)}) custom-call(s32[96]{0:T(128)} %near_rows.1, s32[96]{0:T(128)} %near_sources.1, s32[46]{0:T(128)} %far_rows.1, s32[46]{0:T(128)} %far_sources.1), custom_call_target="tpu_custom_call" | custom-call | tf_op jit(solution)/shard_map/pallas_call | solution.py:443
  4.8 41.0 %shard_map.105 = (f32[16,4096]{1,0:T(8,128)}, f32[32,16,128]{2,1,0:T(8,128)}, s32[32,128]{1,0:T(8,128)}) custom-call(bf16[16,4096]{1,0:T(8,128)(2,1)} %incident.1, s32[32,128]{1,0:T(8,128)} %bitcast.1, s32[8,1,128]{2,1,0:T(1,128)} %get-tuple-element.7.asks, s32[492]{0:T(512)} %get-tuple-element.8.meta, bf16[96,128,128]{2,1,0:T(8,128)(2,1)} %near_hbm.1, ...), custom_call_target="tpu_custom_call" | custom-call | tf_op jit(solution)/shard_map/pallas_call | solution.py:460
  45.8 10.7 %shard_map.106 = (f32[16,4096]{1,0:T(8,128)}, f32[16,4096]{1,0:T(8,128)}) custom-call(f32[16,4096]{1,0:T(8,128)} %get-tuple-element.9.first_tree, f32[32,16,128]{2,1,0:T(8,128)} %get-tuple-element.10.second_tree, s32[32,128]{1,0:T(8,128)} %get-tuple-element.11.inverse), custom_call_target="tpu_custom_call" | custom-call | tf_op jit(solution)/shard_map/pallas_call | solution.py:513

commit v3 on v2

--- a/solution.py
+++ b/solution.py
@@ -407,15 +407,26 @@
     wait_bytes(all_squares.at[pl.ds(0, owners - 1)], sq_send)
 
 
-def finish(clusters, first_tree, second_tree, inverse, first_image, second_image, sem):
-    copy = pltpu.make_async_copy(first_tree, first_image, sem)
-    copy.start()
+def finish(clusters, first_tree, second_tree, inverse, first_image, second_image, tiles, sems):
+    first = pltpu.make_async_copy(first_tree, first_image, sems.at[CHUNKS])
+    first.start()
+    span = clusters // CHUNKS
+    copies = []
 
     def emit(t, tile):
-        second_image[:, t * 128 : (t + 1) * 128] = tile
+        tiles[:, t * 128 : (t + 1) * 128] = tile
+        if t % span == span - 1:
+            k = t // span
+            columns = pl.ds(k * span * 128, span * 128)
+            copies.append(
+                pltpu.make_async_copy(tiles.at[:, columns], second_image.at[:, columns], sems.at[k])
+            )
+            copies[-1].start()
 
     permute(second_tree, inverse, clusters, emit)
-    copy.wait()
+    first.wait()
+    for copy in copies:
+        copy.wait()
 
 
 def on_device(
@@ -513,9 +524,10 @@
     first, second = pl.pallas_call(
         functools.partial(finish, clusters),
         out_shape=(image, image),
-        in_specs=[anywhere, vmem, vmem],
-        out_specs=(anywhere, vmem),
-        scratch_shapes=[dma],
+        in_specs=[vmem, vmem, vmem],
+        out_specs=(anywhere, anywhere),
+        scratch_shapes=[pltpu.VMEM((ROWS, panels), f32), dma((CHUNKS + 1,))],
+        compiler_params=pltpu.CompilerParams(vmem_limit_bytes=16 * 2**20),
     )(first, second, inverse)
     return first[:headings], second[:headings]
 

time: 56.7 us -> 51.7 us (0.912)
  Pallas kernels: 55.9 us -> 48.2 us
  local copies, waits for them, and re-layouts: 0 us -> 2.61 us
    pallas_call x1, Pallas kernels: 10.7 us -> 3 us  [on_device(): pl.pallas_call(functools.partial(finish, clusters), out_shape=(image, ima...]
    unnamed x0 -> x6, local copies, waits for them, and re-layouts: none -> 2.61 us
where the time goes in v3:
time: 51.7 us; the launch traced here: 51.5 us
  Pallas kernels  48.2 us (93%)
  local copies, waits for them, and re-layouts  2.61 us (5%)
  between operations  0.66 us (1%)
    pallas_call x1, Pallas kernels, on_device(): pl.pallas_call(functools.partial(kernel, clusters, owners, shares, near,...  41 us
    pallas_call x1, Pallas kernels, on_device(): pl.pallas_call(functools.partial(prepare, clusters, owners), out_shape=(j...  4.17 us
    pallas_call x1, Pallas kernels, on_device(): pl.pallas_call(functools.partial(finish, clusters), out_shape=(image, ima...  3 us
    unnamed x6, local copies, waits for them, and re-layouts  2.61 us

profile of v3, /device:TPU:0, one launch (start us, length us, event | category | flops | bytes accessed | tf_op | source)
XLA Modules:
  0.0 51.5 jit_solution(6496934814861702119)
XLA Ops:
  0.6 4.2 %shard_map.104 = (s32[492]{0:T(512)}, s32[8,1,128]{2,1,0:T(1,128)}) custom-call(s32[96]{0:T(128)} %near_rows.1, s32[96]{0:T(128)} %near_sources.1, s32[46]{0:T(128)} %far_rows.1, s32[46]{0:T(128)} %far_sources.1), custom_call_target="tpu_custom_call" | custom-call | tf_op jit(solution)/shard_map/pallas_call | solution.py:454
  4.8 41.0 %shard_map.105 = (f32[16,4096]{1,0:T(8,128)}, f32[32,16,128]{2,1,0:T(8,128)}, s32[32,128]{1,0:T(8,128)}) custom-call(bf16[16,4096]{1,0:T(8,128)(2,1)} %incident.1, s32[32,128]{1,0:T(8,128)} %bitcast.1, s32[8,1,128]{2,1,0:T(1,128)} %get-tuple-element.7.asks, s32[492]{0:T(512)} %get-tuple-element.8.meta, bf16[96,128,128]{2,1,0:T(8,128)(2,1)} %near_hbm.1, ...), custom_call_target="tpu_custom_call" | custom-call | tf_op jit(solution)/shard_map/pallas_call | solution.py:471
  45.8 0.0 copy-start
  45.9 0.9 %copy-done = f32[16,4096]{1,0:T(8,128)S(1)} copy-done((f32[16,4096]{1,0:T(8,128)S(1)}, f32[16,4096]{1,0:T(8,128)}, u32[]{:S(2)}) %copy-start) | copy-done | bytes 262168
  46.8 0.0 copy-start.1
  46.8 0.9 %copy-done.1 = f32[32,16,128]{2,1,0:T(8,128)S(1)} copy-done((f32[32,16,128]{2,1,0:T(8,128)S(1)}, f32[32,16,128]{2,1,0:T(8,128)}, u32[]{:S(2)}) %copy-start.1) | copy-done | bytes 262168
  47.7 0.0 copy-start.2
  47.8 0.7 %copy-done.2 = s32[32,128]{1,0:T(8,128)S(1)} copy-done((s32[32,128]{1,0:T(8,128)S(1)}, s32[32,128]{1,0:T(8,128)}, u32[]{:S(2)}) %copy-start.2) | copy-done | bytes 16408
  48.5 3.0 %shard_map.106 = (f32[16,4096]{1,0:T(8,128)}, f32[16,4096]{1,0:T(8,128)}) custom-call(f32[16,4096]{1,0:T(8,128)S(1)} %copy-done, f32[32,16,128]{2,1,0:T(8,128)S(1)} %copy-done.1, s32[32,128]{1,0:T(8,128)S(1)} %copy-done.2), custom_call_target="tpu_custom_call" | custom-call | tf_op jit(solution)/shard_map/pallas_call | solution.py:524
Async XLA Ops:
  45.8 1.0 %copy-start = (f32[16,4096]{1,0:T(8,128)S(1)}, f32[16,4096]{1,0:T(8,128)}, u32[]{:S(2)}) copy-start(f32[16,4096]{1,0:T(8,128)} %get-tuple-element.9.first_tree) | copy-start | bytes 786436
  46.8 0.9 %copy-start.1 = (f32[32,16,128]{2,1,0:T(8,128)S(1)}, f32[32,16,128]{2,1,0:T(8,128)}, u32[]{:S(2)}) copy-start(f32[32,16,128]{2,1,0:T(8,128)} %get-tuple-element.10.second_tree) | copy-start | bytes 786436
  47.7 0.7 %copy-start.2 = (s32[32,128]{1,0:T(8,128)S(1)}, s32[32,128]{1,0:T(8,128)}, u32[]{:S(2)}) copy-start(s32[32,128]{1,0:T(8,128)} %get-tuple-element.11.inverse) | copy-start | bytes 49156

commit v4 on v3

--- a/solution.py
+++ b/solution.py
@@ -29,7 +29,7 @@
         cnt[r] = cnt[r] + 1
         return 0
 
-    lax.fori_loop(0, count, tally, 0, unroll=2)
+    lax.fori_loop(0, count, tally, 0, unroll=8)
 
     def prefix(c, run):
         n = cnt[c]
@@ -38,7 +38,7 @@
         meta[end + c] = jnp.where(n > 0, run + n - 1, count)
         return run + n
 
-    lax.fori_loop(0, clusters + 1, prefix, 0, unroll=3)
+    lax.fori_loop(0, clusters + 1, prefix, 0, unroll=True)
 
     def place(e, _):
         r = rows_ref[e]
@@ -49,7 +49,7 @@
         meta[keep + pos] = jnp.where(pos == start[r], 0, 1)
         return 0
 
-    lax.fori_loop(0, count, place, 0, unroll=2)
+    lax.fori_loop(0, count, place, 0, unroll=8)
     return end + clusters + 1
 
 
@@ -407,9 +407,15 @@
     wait_bytes(all_squares.at[pl.ds(0, owners - 1)], sq_send)
 
 
-def finish(clusters, first_tree, second_tree, inverse, first_image, second_image, tiles, sems):
-    first = pltpu.make_async_copy(first_tree, first_image, sems.at[CHUNKS])
-    first.start()
+def finish(
+    clusters, first_hbm, second_hbm, inverse_hbm, first_image, second_image, first, tree, inverse, tiles, sems
+):
+    loads = [
+        pltpu.make_async_copy(src, dst, sems.at[CHUNKS + k])
+        for k, (src, dst) in enumerate(((inverse_hbm, inverse), (second_hbm, tree), (first_hbm, first)))
+    ]
+    for load in loads:
+        load.start()
     span = clusters // CHUNKS
     copies = []
 
@@ -423,8 +429,12 @@
             )
             copies[-1].start()
 
-    permute(second_tree, inverse, clusters, emit)
-    first.wait()
+    loads[0].wait()
+    loads[1].wait()
+    permute(tree, inverse, clusters, emit)
+    loads[2].wait()
+    copies.append(pltpu.make_async_copy(first, first_image, sems.at[CHUNKS + 3]))
+    copies[-1].start()
     for copy in copies:
         copy.wait()
 
@@ -524,10 +534,16 @@
     first, second = pl.pallas_call(
         functools.partial(finish, clusters),
         out_shape=(image, image),
-        in_specs=[vmem, vmem, vmem],
+        in_specs=[anywhere, anywhere, anywhere],
         out_specs=(anywhere, anywhere),
-        scratch_shapes=[pltpu.VMEM((ROWS, panels), f32), dma((CHUNKS + 1,))],
-        compiler_params=pltpu.CompilerParams(vmem_limit_bytes=16 * 2**20),
+        scratch_shapes=[
+            pltpu.VMEM((ROWS, panels), f32),
+            pltpu.VMEM((clusters, ROWS, block), f32),
+            pltpu.VMEM((clusters, block), jnp.int32),
+            pltpu.VMEM((ROWS, panels), f32),
+            dma((CHUNKS + 4,)),
+        ],
+        compiler_params=pltpu.CompilerParams(vmem_limit_bytes=56 * 2**20),
     )(first, second, inverse)
     return first[:headings], second[:headings]
 

time: 51.7 us -> 49.5 us (0.957)
  local copies, waits for them, and re-layouts: 2.61 us -> 0 us
    unnamed x6 -> x0, local copies, waits for them, and re-layouts: 2.61 us -> none
    pallas_call x1, Pallas kernels: 3 us -> 4.09 us  [on_device(): pl.pallas_call(functools.partial(finish, clusters), out_shape=(image, ima...]
    pallas_call x1, Pallas kernels: 4.17 us -> 3.53 us  [on_device(): pl.pallas_call(functools.partial(prepare, clusters, owners), out_shape=(j...]
where the time goes in v4:
time: 49.5 us; the launch traced here: 49.3 us
  Pallas kernels  48.7 us (98%)
  between operations  0.65 us (1%)
    pallas_call x1, Pallas kernels, on_device(): pl.pallas_call(functools.partial(kernel, clusters, owners, shares, near,...  41 us
    pallas_call x1, Pallas kernels, on_device(): pl.pallas_call(functools.partial(finish, clusters), out_shape=(image, ima...  4.09 us
    pallas_call x1, Pallas kernels, on_device(): pl.pallas_call(functools.partial(prepare, clusters, owners), out_shape=(j...  3.53 us

profile of v4, /device:TPU:0, one launch (start us, length us, event | category | flops | bytes accessed | tf_op | source)
XLA Modules:
  0.0 49.3 jit_solution(12152235850974415274)
XLA Ops:
  0.6 3.5 %shard_map.104 = (s32[492]{0:T(512)}, s32[8,1,128]{2,1,0:T(1,128)}) custom-call(s32[96]{0:T(128)} %near_rows.1, s32[96]{0:T(128)} %near_sources.1, s32[46]{0:T(128)} %far_rows.1, s32[46]{0:T(128)} %far_sources.1), custom_call_target="tpu_custom_call" | custom-call | tf_op jit(solution)/shard_map/pallas_call | solution.py:464
  4.2 41.0 %shard_map.105 = (f32[16,4096]{1,0:T(8,128)}, f32[32,16,128]{2,1,0:T(8,128)}, s32[32,128]{1,0:T(8,128)}) custom-call(bf16[16,4096]{1,0:T(8,128)(2,1)} %incident.1, s32[32,128]{1,0:T(8,128)} %bitcast.1, s32[8,1,128]{2,1,0:T(1,128)} %get-tuple-element.7.asks, s32[492]{0:T(512)} %get-tuple-element.8.meta, bf16[96,128,128]{2,1,0:T(8,128)(2,1)} %near_hbm.1, ...), custom_call_target="tpu_custom_call" | custom-call | tf_op jit(solution)/shard_map/pallas_call | solution.py:481
  45.2 4.1 %shard_map.106 = (f32[16,4096]{1,0:T(8,128)}, f32[16,4096]{1,0:T(8,128)}) custom-call(f32[16,4096]{1,0:T(8,128)} %get-tuple-element.9.first_hbm, f32[32,16,128]{2,1,0:T(8,128)} %get-tuple-element.10.second_hbm, s32[32,128]{1,0:T(8,128)} %get-tuple-element.11.inverse_hbm), custom_call_target="tpu_custom_call" | custom-call | tf_op jit(solution)/shard_map/pallas_call | solution.py:534
